TPU v7x, 128 devices: a whole 4x4x4 slice. The times are simulated.
128 devices in a mesh: row: 64 (over z, y, x), mode: 2 (over core).
Axes of the slice: x: 4, y: 4, z: 4, core: 2. Of those that a mesh axis runs over, the one named last changes fastest.
Arguments:
- eigenvectors: float32 [131072, 1024], P('row', 'mode'), may hold values from -6 to 6
- reflectors: float32 [4, 131072, 256], P(None, 'row'), may hold values from -0.015625 to 0.015625
- factors: float32 [4, 256, 256], replicated, as said below
- dof_index: int32 [12, 65536], P(None, 'row'), may hold values from 0 to 131071, as said below
- stiffness: float32 [4, 12, 65536], P(None, None, 'row'), may hold values from -6 to 6
- frequency: float32 [1024], replicated, may hold values from 1 to 60
- amplitude: float32 [1024], P('mode'), may hold values from -0.2 to 0.2
- capacity: float32 [4, 65536], P(None, ('row', 'mode')), may hold values from 2 to 20
- section_ratio: float32 [65536], P(('row', 'mode')), may hold values from 0.5 to 2
Outputs:
- mode_shapes: float32 [131072, 1024], P('row', 'mode')
- demand: float32 [4, 65536], P(None, ('row', 'mode'))
- resized: float32 [65536], P(('row', 'mode'))
Inputs may be any that keep to these rules, and one draw needn't show every extreme that they name: `dof_index`: every entry for member e, with d = e // 1024, lies in rows d * 2048 to d * 2048 + 2303, and every block but the last reaches that end. `factors`: upper triangular; nothing below the diagonal.
All inputs are finite; a program needn't handle non-finite values.
Results may differ from a plain program's by a relative error of at most 0.0016.
Values may be sent and summed in bfloat16 or wider, within the bound.
No kernel may reach another device: no remote copies, remote signals or barrier semaphores. Data moves between devices by JAX's collectives and lax.ppermute only.
A program may use at most 128 MiB of HBM per device.

v0:
```python
import jax
import jax.numpy as jnp
from jax import lax
from jax.sharding import PartitionSpec as P

PANELS = 4
HALO = 256


damping_ratio = 0.05


def passed_along(x, axis, by):
    count = lax.axis_size(axis)
    pairs = [(i, i + by) for i in range(count) if 0 <= i + by < count]
    return lax.ppermute(x, axis, pairs)


def correlation(frequency):
    freq_ratio = frequency[None, :] / frequency[:, None]
    squared = damping_ratio * damping_ratio
    numerator = 8.0 * squared * (1.0 + freq_ratio) * freq_ratio * jnp.sqrt(freq_ratio)
    denominator = (1.0 - freq_ratio * freq_ratio) ** 2 + 4.0 * squared * freq_ratio * (
        1.0 + freq_ratio
    ) ** 2
    return (numerator / denominator).astype(jnp.bfloat16)


def shards(
    eigenvectors,
    reflectors,
    factors,
    dof_index,
    stiffness,
    frequency,
    amplitude,
    capacity,
    section_ratio,
):
    highest = lax.Precision.HIGHEST
    vectors = eigenvectors
    for panel in reversed(range(PANELS)):
        partial_sum = jnp.einsum("rb,rm->bm", reflectors[panel], vectors, precision=highest)
        projection = lax.psum(partial_sum, "row")
        applied = jnp.dot(factors[panel], projection, precision=highest)
        vectors = vectors - jnp.dot(reflectors[panel], applied, precision=highest)
    border_rows = passed_along(vectors[:HALO], "row", -1)
    extended = jnp.concatenate([vectors, border_rows], axis=0)
    first_row = lax.axis_index("row") * vectors.shape[0]
    local_index = dof_index - first_row
    picked = jnp.take(extended, local_index, axis=0)
    member_force = jnp.einsum("cke,kem->cem", stiffness, picked, precision=highest)
    scaled = (member_force * amplitude[None, None, :]).astype(jnp.bfloat16)
    weights_table = correlation(frequency)
    member_block = lax.all_to_all(scaled, "mode", split_axis=1, concat_axis=2, tiled=True)
    weighted = jnp.einsum(
        "cem,mn->cen", member_block, weights_table, preferred_element_type=jnp.float32
    )
    combined = jnp.sum(member_block * weighted, axis=-1)
    demand = combined / (capacity * capacity)
    resized = section_ratio * jnp.sqrt(0.25 + jnp.sum(demand, axis=0))
    return (vectors, demand, resized)


def solution(mesh):
    in_specs = (
        P("row", "mode"),
        P(None, "row", None),
        P(),
        P(None, "row"),
        P(None, None, "row"),
        P(),
        P("mode"),
        P(None, ("row", "mode")),
        P(("row", "mode")),
    )
    out_specs = (P("row", "mode"), P(None, ("row", "mode")), P(("row", "mode")))
    return jax.shard_map(shards, mesh=mesh, in_specs=in_specs, out_specs=out_specs, check_vma=False)
```

profile of v0, /device:TPU:1, one launch (start us, length us, event | category | flops | bytes accessed | tf_op | source)
XLA Modules:
  0.0 743.9 jit_solution(11929290819760511049)
XLA Ops:
  7.2 7.3 fusion.16
  14.6 5.4 copy.12
  20.0 123.1 %all-reduce.5.cloned.1.call-done = f32[256,512]{1,0:T(8,128)} async-done(((f32[256,512]{1,0:T(8,128)}), f32[256,512]{1,0:T(8,128)}) %all-reduce.5.cloned.1.call-update) | async-done | bytes 524304 | tf_op jit(solution)/shard_map/psum | solution.py:44
  143.1 2.0 fusion.46
  145.2 6.3 bitcast_subtract_fusion.3
  153.5 5.8 fusion.31
  159.7 124.4 %all-reduce.7.cloned.1.call-done = f32[256,512]{0,1:T(8,128)} async-done(((f32[256,512]{0,1:T(8,128)}), f32[256,512]{0,1:T(8,128)}) %all-reduce.7.cloned.1.call-update) | async-done | bytes 524304 | tf_op jit(solution)/shard_map/psum | solution.py:44
  285.8 6.3 bitcast_subtract_fusion.2
  294.1 5.8 fusion.34
  300.5 124.2 %all-reduce.9.cloned.1.call-done = f32[256,512]{0,1:T(8,128)} async-done(((f32[256,512]{0,1:T(8,128)}), f32[256,512]{0,1:T(8,128)}) %all-reduce.9.cloned.1.call-update) | async-done | bytes 524304 | tf_op jit(solution)/shard_map/psum | solution.py:44
  426.4 6.3 bitcast_subtract_fusion.1
  434.7 5.8 fusion.37
  440.6 124.8 %all-reduce.11.cloned.1.call-done = f32[256,512]{0,1:T(8,128)} async-done(((f32[256,512]{0,1:T(8,128)}), f32[256,512]{0,1:T(8,128)}) %all-reduce.11.cloned.1.call-update) | async-done | bytes 524304 | tf_op jit(solution)/shard_map/psum | solution.py:44
  567.1 6.3 bitcast_subtract_fusion
  578.2 5.3 copy.18
  583.6 4.6 collective-permute-done
  588.2 4.7 pad_maximum_fusion
  592.9 6.1 copy.14
  599.0 54.3 %gather_fusion = f32[12288,512]{1,0:T(8,128)} fusion(f32[2304,512]{1,0:T(8,128)} %copy.14, s32[12288]{0:T(1024)S(1)} %broadcast_clamp_fusion), kind=kCustom, calls=%fused_computation | custom fusion | bytes 50380800 | tf_op jit(solution)/shard_map/jit(_take)/gather | solution.py:51
  653.3 49.3 %fusion.3 = bf16[4,1024,512]{2,0,1:T(4,128)(2,1)S(1)} fusion(f32[512]{0:T(512)S(1)} %copy-done.7, f32[4,12,1024]{1,0,2:T(4,128)S(1)} %copy.16, f32[12,1024,512]{2,1,0:T(8,128)} %bitcast.75, pred[12,1024]{0,1:T(8,128)(4,1)S(1)} %copy.13), kind=kOutput, calls=%fused_computation.13 | convolution fusion | flops 312475648 | bytes 29571072 | tf_op jit(solution)/shard_map/cke,kem->cem/dot_general | solution.py:52
  702.6 10.4 %all_to_all.18 = bf16[4,1024,512]{2,0,1:T(4,128)(2,1)S(1)} all-to-all(bf16[4,1024,512]{2,0,1:T(4,128)(2,1)S(1)} %fusion.3), channel_id=1, replica_groups=mesh['row'=64,'mode'=2] {'mode'}, dimensions={1} | all-to-all | bytes 8388608 | tf_op jit(solution)/shard_map/all_to_all | solution.py:55
  713.1 6.2 copy.17
  719.3 7.8 %all_to_all.16 = bf16[4,512,1024]{2,1,0:T(8,128)(2,1)} reshape(bf16[4,512,2,512]{3,2,1,0:T(2,128)(2,1)} %copy.17) | data formatting | bytes 8388608 | tf_op jit(solution)/shard_map/all_to_all | solution.py:55
  727.1 8.8 %multiply_reduce_fusion = f32[4,512]{1,0:T(4,128)S(1)} fusion(bf16[4,512,1024]{2,1,0:T(8,128)(2,1)} %all_to_all.16, f32[1024]{0:T(1024)S(1)} %copy-done.10), kind=kOutput, calls=%fused_computation.5 | convolution fusion | flops 4315936768 | bytes 4206592 | tf_op jit(solution)/shard_map/cem,mn->cen/dot_general | solution.py:56
  (42 shorter events, 18.0 us)
Async XLA Ops:
  7.2 136.0 %all-reduce.5.cloned.1.call-start = ((), (), s32[]{:S(2)}) async-start(), calls=%async_computation.1 | async-start | bytes 1048576 | tf_op jit(solution)/shard_map/psum | solution.py:44
  14.5 128.6 %copy-start.4 = (f32[4,256,256]{2,1,0:T(8,128)S(1)}, f32[4,256,256]{2,1,0:T(8,128)}, u32[]{:S(2)}) copy-start(f32[4,256,256]{2,1,0:T(8,128)} %param.11) | copy-start | bytes 3145732
  14.5 269.6 %all-reduce.7.cloned.1.call-start = ((), (), s32[]{:S(2)}) async-start(), calls=%async_computation.2 | async-start | bytes 1048576 | tf_op jit(solution)/shard_map/psum | solution.py:44
  151.5 2.0 copy-start.2
  159.4 265.4 %all-reduce.9.cloned.1.call-start = ((), (), s32[]{:S(2)}) async-start(), calls=%async_computation.3 | async-start | bytes 1048576 | tf_op jit(solution)/shard_map/psum | solution.py:44
  292.1 2.0 copy-start.3
  300.0 265.4 %all-reduce.11.cloned.1.call-start = ((), (), s32[]{:S(2)}) async-start(), calls=%async_computation.4 | async-start | bytes 1048576 | tf_op jit(solution)/shard_map/psum | solution.py:44
  432.7 2.0 copy-start.1
  567.0 9.9 %copy-start.6 = (s32[12,1024]{1,0:T(8,128)S(1)}, s32[12,1024]{1,0:T(8,128)}, u32[]{:S(2)}) copy-start(s32[12,1024]{1,0:T(8,128)} %param.12) | copy-start | bytes 147460
  567.0 10.3 %copy-start.5 = (f32[4,12,1024]{2,0,1:T(4,128)S(1)}, f32[4,12,1024]{2,0,1:T(4,128)}, u32[]{:S(2)}) copy-start(f32[4,12,1024]{2,0,1:T(4,128)} %param.13) | copy-start | bytes 589828
  573.4 2.0 copy-start
  575.5 12.7 %collective-permute-start = (f32[256,512]{0,1:T(8,128)S(1)}, f32[256,512]{0,1:T(8,128)S(1)}, u32[]{:S(2)}, u32[]{:S(2)}) collective-permute-start(f32[256,512]{0,1:T(8,128)S(1)} %slice.42), channel_id=1, source_target_pairs={{2,0},{4,2},{6,4},{8,6},{10,8},{12,10},{14,12},{16,14},{18,16},{20... | collective-permute-start | bytes 1572872 | tf_op jit(solution)/shard_map/ppermute | solution.py:16
  599.0 54.3 %copy-start.7 = (f32[512]{0:T(512)S(1)}, f32[512]{0:T(512)}, u32[]{:S(2)}) copy-start(f32[512]{0:T(512)} %param.15) | copy-start | bytes 6148
  719.3 7.8 %copy-start.10 = (f32[1024]{0:T(1024)S(1)}, f32[1024]{0:T(1024)}, u32[]{:S(2)}) copy-start(f32[1024]{0:T(1024)} %param.14) | copy-start | bytes 12292
  727.1 8.8 %copy-start.8 = (f32[4,512]{1,0:T(4,128)S(1)}, f32[4,512]{1,0:T(4,128)}, u32[]{:S(2)}) copy-start(f32[4,512]{1,0:T(4,128)} %param.16) | copy-start | bytes 24580
  727.1 9.4 %copy-start.9 = (f32[512]{0:T(512)S(1)}, f32[512]{0:T(512)}, u32[]{:S(2)}) copy-start(f32[512]{0:T(512)} %param.17) | copy-start | bytes 6148
Sparse Core Ops, SparseCore 0:
  14.6 128.4 all-reduce.4
  159.5 124.5 all-reduce.6
  300.1 124.6 all-reduce.8
  440.7 124.6 all-reduce.10
where the time goes:
time: 753 us; the launch traced here: 744 us
  waiting for transfers between devices  501 us (67%)
  matrix products  115 us (15%)
  local copies, waits for them, and re-layouts  94.6 us (13%)
  between operations  14.2 us (2%)
  blocking collectives  10.4 us (1%)
    psum x4, waiting for transfers between devices, shards(): projection = lax.psum(partial_sum, 'row')  496 us
    gather x1, local copies, waits for them, and re-layouts, shards(): picked = jnp.take(extended, local_index, axis=0)  54.3 us
    dot_general x1, matrix products, shards(): jnp.einsum('cke,kem->cem', stiffness, picked, precision=highest)  49.3 us
    dot_general x4, matrix products, shards(): vectors = vectors - jnp.dot(reflectors[panel], applied, precision=highest)  25.3 us
    dot_general x4, matrix products, shards(): jnp.einsum('rb,rm->bm', reflectors[panel], vectors, precision=highest)  24.8 us
    unnamed x25, local copies, waits for them, and re-layouts  19.7 us
  transfers between devices with their start and end apart: 5, of which 5 were waited for; matrix products, arithmetic and copies ran while one was open for 2% of the time, Pallas kernels for 0%

commit v1 on v0

v1 whole, which is shorter than its diff:
```python
import functools

import jax
import jax.numpy as jnp
from jax import lax
from jax.experimental import pallas as pl
from jax.experimental.pallas import tpu as pltpu
from jax.sharding import PartitionSpec as P

PANELS = 4
COLS = 256
HALO = 256
MEM_DOFS = 12
COMPS = 4
MODES = 1024
LANES = 128
bf16 = jnp.bfloat16
f32 = jnp.float32
VMEM_LIMIT = 58 * 1024 * 1024

damping_ratio = 0.05
PAIRS = (((0, 3), (1, 3), (2, 3)), ((0, 2), (1, 2), (0, 1)))


def contract_rows(a, b):
    return lax.dot_general(a, b, (((0,), (0,)), ((), ())), preferred_element_type=f32)


def mm(a, b):
    return jnp.dot(a, b, preferred_element_type=f32)


def project_kernel(core_ref, refl_ref, vec_ref, out_ref, half_ref, proj, gram):
    step = pl.program_id(0)

    @pl.when(step == 0)
    def _():
        proj[...] = jnp.zeros_like(proj)
        gram[...] = jnp.zeros_like(gram)

    vec = vec_ref[...].astype(bf16)
    half_ref[...] = vec
    refl = jnp.concatenate([refl_ref[p].astype(bf16) for p in range(PANELS)], axis=1)

    proj[...] += contract_rows(vec, refl)

    @pl.when(core_ref[0] == 0)
    def _():
        gram[...] += contract_rows(refl[:, 3 * COLS :], refl[:, : 3 * COLS])

    @pl.when(core_ref[0] == 1)
    def _():
        gram[:, : 2 * COLS] += contract_rows(refl[:, 2 * COLS : 3 * COLS], refl[:, : 2 * COLS])
        gram[:, 2 * COLS :] += contract_rows(refl[:, COLS : 2 * COLS], refl[:, :COLS])

    @pl.when(step == pl.num_programs(0) - 1)
    def _():
        rows = PANELS * COLS
        parts = proj.shape[0] // LANES
        for m in range(parts):
            out_ref[m * rows : (m + 1) * rows] = proj[m * LANES : (m + 1) * LANES].T.astype(bf16)
        start = parts * rows
        for m in range(COLS // LANES):
            out_ref[start : start + 3 * COLS] = gram[m * LANES : (m + 1) * LANES].T.astype(bf16)
            start += 3 * COLS


def project(core, reflectors, vectors):
    rows, cols = vectors.shape
    chunk = 512
    out_rows = (cols // LANES) * PANELS * COLS + (COLS // LANES) * 3 * COLS
    return pl.pallas_call(
        project_kernel,
        grid=(rows // chunk,),
        in_specs=[
            pl.BlockSpec(memory_space=pltpu.SMEM),
            pl.BlockSpec((PANELS, chunk, COLS), lambda i: (0, i, 0)),
            pl.BlockSpec((chunk, cols), lambda i: (i, 0)),
        ],
        out_specs=[
            pl.BlockSpec((out_rows, LANES), lambda i: (0, 0)),
            pl.BlockSpec((chunk, cols), lambda i: (i, 0)),
        ],
        out_shape=[
            jax.ShapeDtypeStruct((out_rows, LANES), bf16),
            jax.ShapeDtypeStruct((rows, cols), bf16),
        ],
        scratch_shapes=[pltpu.VMEM((cols, PANELS * COLS), f32), pltpu.VMEM((COLS, 3 * COLS), f32)],
        compiler_params=pltpu.CompilerParams(vmem_limit_bytes=VMEM_LIMIT),
        cost_estimate=pl.CostEstimate(flops=4 * rows * 256 * 512 * 4, bytes_accessed=14 << 20, transcendentals=0),
        name="project",
    )(core, reflectors, vectors)


def top_kernel(core_ref, vec_ref, refl_ref, out_ref):
    out_ref[:HALO] = vec_ref[...].astype(bf16)
    for h in range(2):
        out_ref[HALO:, h * COLS : (h + 1) * COLS] = refl_ref[2 * core_ref[0] + h].astype(bf16)


def top_rows(core, vectors, reflectors):
    cols = vectors.shape[1]
    return pl.pallas_call(
        top_kernel,
        grid=(1,),
        in_specs=[
            pl.BlockSpec(memory_space=pltpu.SMEM),
            pl.BlockSpec((HALO, cols), lambda i: (0, 0)),
            pl.BlockSpec((PANELS, HALO, COLS), lambda i: (0, 0, 0)),
        ],
        out_specs=pl.BlockSpec((2 * HALO, cols), lambda i: (0, 0)),
        out_shape=jax.ShapeDtypeStruct((2 * HALO, cols), bf16),
        name="top_rows",
    )(core, vectors, reflectors)


GROUP = 128
FILL = 1024
TERMS = COMPS * MEM_DOFS
AT_ONCE = 16


def lay_out(table, first, slot, block):
    table[pl.ds(first * 8 + slot, block.shape[0], stride=8), :] = block.astype(f32)


def strip(s):
    return slice(s * LANES, (s + 1) * LANES)


def spread_coefs(stiff_ref, wide):
    stiff = stiff_ref[...]
    high = stiff.astype(bf16)
    low = (stiff - high.astype(f32)).astype(bf16)
    both = jnp.concatenate([high, low], axis=1)
    lane = lax.broadcasted_iota(jnp.int32, (1, 2 * GROUP), 1) % GROUP
    ones = jnp.ones((2 * GROUP, LANES), bf16)
    for start in range(0, GROUP, AT_ONCE):
        picked = [
            both * jnp.where(lane == e, 1.0, 0.0).astype(bf16) for e in range(start, start + AT_ONCE)
        ]
        wide[start * TERMS : (start + AT_ONCE) * TERMS] = mm(jnp.concatenate(picked, axis=0), ones)


def member_rows(index_ref, stiff_ref, table, wide, sums, out_ref, step, members):
    spread_coefs(stiff_ref, wide)

    def one(i, _):
        e = step * GROUP + i
        stiff = wide[pl.ds(pl.multiple_of(i * TERMS, 8), TERMS), :]
        acc = [None] * COMPS
        for k in range(MEM_DOFS):
            at = pl.multiple_of(index_ref[k * members + e], 8)
            row = table[pl.ds(at, 8), :]
            for c in range(COMPS):
                j = c * MEM_DOFS + k
                term = stiff[j : j + 1] * row
                acc[c] = term if k == 0 else acc[c] + term
        for c in range(COMPS):
            sums[pl.ds(pl.multiple_of((c * GROUP + i) * 8, 8), 8), :] = acc[c]
        return 0

    lax.fori_loop(0, GROUP, one, 0, unroll=8)
    for c in range(COMPS):
        for s in range(8):
            out_ref[c, :, strip(s)] = sums[pl.ds(c * GROUP * 8 + s, GROUP, stride=8), :].astype(out_ref.dtype)


def refl_kernel(members, core_ref, index_ref, stiff_ref, refl_ref, halo_ref, end_ref, out_ref, flat_ref, table, wide, sums):
    step = pl.program_id(0)
    rows = table.shape[0] // 8 - HALO
    fills = rows // FILL

    @pl.when(step < fills)
    def _():
        for s in range(8):
            lay_out(table, step * FILL, s, refl_ref[s // 2, :, strip(s % 2)])
        for p in range(PANELS):
            flat_ref[:, p * COLS : (p + 1) * COLS] = refl_ref[p].astype(bf16)

    @pl.when(step == fills)
    def _():
        core = core_ref[0]
        for s in range(4):
            lay_out(table, rows, s + 4 * core, halo_ref[HALO:, strip(s)])
            lay_out(table, rows, s + 4 * (1 - core), end_ref[HALO : 2 * HALO, strip(s)])

    @pl.when(step >= fills)
    def _():
        member_rows(index_ref, stiff_ref, table, wide, sums, out_ref, step - fills, members)


def vec_kernel(members, core_ref, index_ref, stiff_ref, vec_ref, other_ref, halo_ref, end_ref, out_ref, table, wide, sums):
    step = pl.program_id(0)
    rows = table.shape[0] // 8 - HALO
    fills = rows // FILL

    @pl.when(step < fills)
    def _():
        for s in range(4):
            lay_out(table, step * FILL, s, vec_ref[:, strip(s)])
            lay_out(table, step * FILL, 4 + s, other_ref[:, strip(s)])

    @pl.when(step == fills)
    def _():
        for s in range(4):
            lay_out(table, rows, s, halo_ref[:HALO, strip(s)])
            lay_out(table, rows, 4 + s, end_ref[:HALO, strip(s)])

    @pl.when(step >= fills)
    def _():
        member_rows(index_ref, stiff_ref, table, wide, sums, out_ref, step - fills, members)


def gather(kernel, name, rows, core, index, stiff, blocks, block_specs, out_shape, flat=False):
    members = stiff.shape[1]
    fills = rows // FILL
    smem = pl.BlockSpec(memory_space=pltpu.SMEM)
    fill_at = lambda i: jnp.minimum(i, fills - 1)
    group_at = lambda i: jnp.maximum(i - fills, 0)
    whole = lambda i: (0, 0)
    out_specs = [pl.BlockSpec((COMPS, GROUP, MODES), lambda i: (0, group_at(i), 0))]
    if flat:
        out_specs.append(pl.BlockSpec((FILL, MODES), lambda i: (fill_at(i), 0)))
    return pl.pallas_call(
        functools.partial(kernel, members),
        grid=(fills + members // GROUP,),
        in_specs=[smem, smem, pl.BlockSpec((TERMS, GROUP), lambda i: (0, group_at(i)))]
        + [spec(fill_at) for spec in block_specs]
        + [pl.BlockSpec((2 * HALO, MODES // 2), whole), pl.BlockSpec((2 * HALO + 16, MODES // 2), whole)],
        out_specs=out_specs,
        out_shape=out_shape,
        scratch_shapes=[
            pltpu.VMEM(((rows + HALO) * 8, LANES), f32),
            pltpu.VMEM((TERMS * GROUP, LANES), f32),
            pltpu.VMEM((COMPS * GROUP * 8, LANES), f32),
        ],
        compiler_params=pltpu.CompilerParams(vmem_limit_bytes=VMEM_LIMIT),
        cost_estimate=pl.CostEstimate(flops=1 << 20, bytes_accessed=1 << 20, transcendentals=0),
        name=name,
    )(core, index, stiff, *blocks)


def gather_reflectors(core, index, stiff, reflectors, halo, end):
    rows = reflectors.shape[1]
    return gather(
        refl_kernel,
        "gather_reflectors",
        rows,
        core,
        index,
        stiff,
        (reflectors, halo, end),
        [lambda at: pl.BlockSpec((PANELS, FILL, COLS), lambda i: (0, at(i), 0))],
        [
            jax.ShapeDtypeStruct((COMPS, stiff.shape[1], MODES), bf16),
            jax.ShapeDtypeStruct((rows, MODES), bf16),
        ],
        flat=True,
    )


def gather_vectors(core, index, stiff, vectors, other, halo, end):
    rows, cols = vectors.shape
    spec = lambda at: pl.BlockSpec((FILL, cols), lambda i: (at(i), 0))
    return gather(
        vec_kernel,
        "gather_vectors",
        rows,
        core,
        index,
        stiff,
        (vectors, other, halo, end),
        [spec, spec],
        [jax.ShapeDtypeStruct((COMPS, stiff.shape[1], MODES), f32)],
    )[0]


def solve_panels(first, second, mine_ref, other_ref, factor_ref, coef):
    rows = PANELS * COLS
    parts = coef.shape[1] // 2 // LANES
    blocks = {}
    for ref, pairs in ((first, PAIRS[0]), (second, PAIRS[1])):
        for i, pair in enumerate(pairs):
            start = parts * rows + i * COLS
            blocks[pair] = jnp.concatenate(
                [ref[start : start + COLS], ref[start + 3 * COLS : start + 4 * COLS]], axis=1
            )
    for p in reversed(range(PANELS)):
        factor = factor_ref[p]
        high = factor.astype(bf16)
        low = (factor - high.astype(f32)).astype(bf16)
        now = jnp.concatenate(
            [
                ref[m * rows + p * COLS : m * rows + (p + 1) * COLS]
                for ref in (mine_ref, other_ref)
                for m in range(parts)
            ],
            axis=1,
        ).astype(f32)
        if p < PANELS - 1:
            gram = jnp.concatenate([blocks[(p, q)] for q in range(p + 1, PANELS)], axis=1)
            now = now - mm(gram, coef[(p + 1) * COLS :])
        now_high = now.astype(bf16)
        now_low = (now - now_high.astype(f32)).astype(bf16)
        coef[p * COLS : (p + 1) * COLS] = (
            mm(high, now_high) + (mm(low, now_high) + mm(high, now_low))
        ).astype(bf16)


def finish_kernel(
    core_ref, mine_ref, other_ref, factor_ref, vec_ref, flat_ref, force_ref, refl_ref, weight_ref, amp_ref,
    cap_ref, ratio_ref, out_ref, demand_ref, resized_ref, coef,
):
    step = pl.program_id(0)
    for core in range(2):

        @pl.when((step == 0) & (core_ref[0] == core))
        def _():
            pair = (mine_ref, other_ref) if core == 0 else (other_ref, mine_ref)
            solve_panels(*pair, mine_ref, other_ref, factor_ref, coef)

    @pl.when(step > 0)
    def _():
        group = force_ref.shape[1]
        force = force_ref[...].reshape(COMPS * group, MODES)
        force = force - mm(refl_ref[...].reshape(COMPS * group, MODES), coef[...])
        scaled = (force * amp_ref[...]).astype(bf16)
        part = None
        for b in range(MODES // COLS):
            upto = (b + 1) * COLS
            here = slice(b * COLS, upto)
            weighted = mm(scaled[:, here], weight_ref[here, here])
            if b > 0:
                weighted = weighted + 2.0 * mm(scaled[:, : b * COLS], weight_ref[: b * COLS, here])
            product = weighted * scaled[:, b * COLS : upto].astype(f32)
            both = product[:, :LANES] + product[:, LANES:]
            part = both if part is None else part + both
        total = jnp.full((1, group), 0.25, f32)
        for c in range(COMPS):
            combined = jnp.sum(part[c * group : (c + 1) * group].T, axis=0, keepdims=True)
            capacity = cap_ref[c : c + 1]
            demand = combined / (capacity * capacity)
            demand_ref[c : c + 1] = demand
            total = total + demand
        resized_ref[...] = ratio_ref[...] * jnp.sqrt(total)
        out_ref[...] = vec_ref[...] - mm(flat_ref[...], coef[:, : out_ref.shape[1]])


def finish(core, mine, other, factors, vectors, flat, from_vec, from_refl, weights, amp, capacity, ratio):
    members = from_vec.shape[1]
    rows, cols = vectors.shape
    group = 128
    steps = members // group
    chunk = rows // steps
    whole = pl.BlockSpec(memory_space=pltpu.VMEM)
    at = lambda i: jnp.maximum(i - 1, 0)
    return pl.pallas_call(
        finish_kernel,
        grid=(1 + steps,),
        in_specs=[
            pl.BlockSpec(memory_space=pltpu.SMEM),
            whole,
            whole,
            whole,
            pl.BlockSpec((chunk, cols), lambda i: (at(i), 0)),
            pl.BlockSpec((chunk, MODES), lambda i: (at(i), 0)),
            pl.BlockSpec((COMPS, group, MODES), lambda i: (0, at(i), 0)),
            pl.BlockSpec((COMPS, group, MODES), lambda i: (0, at(i), 0)),
            whole,
            whole,
            pl.BlockSpec((COMPS, group), lambda i: (0, at(i))),
            pl.BlockSpec((1, group), lambda i: (0, at(i))),
        ],
        out_specs=[
            pl.BlockSpec((chunk, cols), lambda i: (at(i), 0)),
            pl.BlockSpec((COMPS, group), lambda i: (0, at(i))),
            pl.BlockSpec((1, group), lambda i: (0, at(i))),
        ],
        out_shape=[
            jax.ShapeDtypeStruct((rows, cols), f32),
            jax.ShapeDtypeStruct((COMPS, members), f32),
            jax.ShapeDtypeStruct((1, members), f32),
        ],
        scratch_shapes=[pltpu.VMEM((PANELS * COLS, MODES), bf16)],
        compiler_params=pltpu.CompilerParams(vmem_limit_bytes=VMEM_LIMIT),
        cost_estimate=pl.CostEstimate(flops=12 << 30, bytes_accessed=30 << 20, transcendentals=0),
        name="finish",
    )(core, mine, other, factors, vectors, flat, from_vec, from_refl, weights, amp, capacity, ratio)


def correlation(frequency):
    freq_ratio = frequency[None, :] / frequency[:, None]
    squared = damping_ratio * damping_ratio
    numerator = 8.0 * squared * (1.0 + freq_ratio) * freq_ratio * jnp.sqrt(freq_ratio)
    denominator = (1.0 - freq_ratio * freq_ratio) ** 2 + 4.0 * squared * freq_ratio * (
        1.0 + freq_ratio
    ) ** 2
    return (numerator / denominator).astype(bf16)


def shards(
    eigenvectors,
    reflectors,
    factors,
    dof_index,
    stiffness,
    frequency,
    amplitude,
    capacity,
    section_ratio,
):
    row_count = lax.axis_size("row")
    core = lax.axis_index("mode")
    core_arr = core.astype(jnp.int32).reshape(1)
    rows, cols = eigenvectors.shape
    members = capacity.shape[1]
    swap = [(0, 1), (1, 0)]

    top = top_rows(core_arr, eigenvectors, reflectors)
    halo = lax.ppermute(top, "row", [(i + 1, i) for i in range(row_count - 1)])
    _, reflectors_after = lax.optimization_barrier((top, reflectors))
    partial_sums, half = project(core_arr, reflectors_after, eigenvectors)
    partial_sums, halo = lax.optimization_barrier((partial_sums, halo))
    shard = partial_sums.shape[0] // row_count
    pieces = lax.all_to_all(
        partial_sums.reshape(row_count, shard, LANES), "row", split_axis=0, concat_axis=0, tiled=True
    )

    other = lax.ppermute(half, "mode", swap)
    amp_high = amplitude.astype(bf16)
    amp_rest = amplitude - amp_high.astype(f32)
    amp_mid = amp_rest.astype(bf16)
    amp_low = (amp_rest - amp_mid.astype(f32)).astype(bf16)
    amp_rows = jnp.concatenate(
        [amp_high[None], amp_mid[None], amp_low[None], jnp.zeros((13, cols), bf16)], axis=0
    )
    end = lax.ppermute(jnp.concatenate([halo, amp_rows], axis=0), "mode", swap)
    amp_other = jnp.sum(end[2 * HALO : 2 * HALO + 3].astype(f32), axis=0)
    amp_all = jnp.concatenate([amplitude, amp_other])[None]

    first_row = lax.axis_index("row") * rows
    index = lax.dynamic_slice_in_dim(dof_index, core * members, members, axis=1)
    index = ((index - first_row) * 8).reshape(-1)
    stiff = lax.dynamic_slice_in_dim(stiffness, core * members, members, axis=2)
    stiff = stiff.reshape(TERMS, members)
    from_refl, flat = gather_reflectors(core_arr, index, stiff, reflectors, halo, end)
    pieces, from_refl, flat = lax.optimization_barrier((pieces, from_refl, flat))
    summed = jnp.sum(pieces.astype(f32), axis=0).astype(bf16)
    summed, frequency, index = lax.optimization_barrier((summed, frequency, index))
    spread = lax.all_to_all(
        jnp.broadcast_to(summed[None], (row_count, shard, LANES)), "row", split_axis=0, concat_axis=0, tiled=True
    )
    from_vec = gather_vectors(core_arr, index, stiff, eigenvectors, other, halo, end)

    freq_halves = frequency.reshape(2, cols)
    freq_all = jnp.where(core == 0, freq_halves, freq_halves[::-1]).reshape(-1)
    weights_table = correlation(freq_all)

    spread, from_vec, weights_table = lax.optimization_barrier((spread, from_vec, weights_table))
    sums_mine = spread.reshape(row_count * shard, LANES)
    sums_other = lax.ppermute(sums_mine, "mode", swap)
    vectors, demand, resized = finish(
        core_arr, sums_mine, sums_other, factors, eigenvectors, flat, from_vec, from_refl, weights_table,
        amp_all, capacity, section_ratio[None],
    )
    return (vectors, demand, resized.reshape(-1))


def solution(mesh):
    in_specs = (
        P("row", "mode"),
        P(None, "row", None),
        P(),
        P(None, "row"),
        P(None, None, "row"),
        P(),
        P("mode"),
        P(None, ("row", "mode")),
        P(("row", "mode")),
    )
    out_specs = (P("row", "mode"), P(None, ("row", "mode")), P(("row", "mode")))
    return jax.shard_map(shards, mesh=mesh, in_specs=in_specs, out_specs=out_specs, check_vma=False)
```

time: 753 us -> 124 us (0.16); the launches traced: 744 us -> 124 us
  waiting for transfers between devices: 501 us -> 8.71 us
  matrix products: 115 us -> 0 us
  local copies, waits for them, and re-layouts: 94.6 us -> 5.04 us
  Pallas kernels: 0 us -> 73.9 us
  starting transfers between devices: 2.45 us -> 29.6 us
  between operations: 14.2 us -> 0.93 us
  blocking collectives: 10.4 us -> 0 us
    psum x4 -> x0, waiting for transfers between devices: 496 us -> none  [shards(): projection = lax.psum(partial_sum, 'row')]
    dot_general x14 -> x0, matrix products: 115 us -> none  [the longest x1 49.3 us: shards(): jnp.einsum('cke,kem->cem', stiffness, picked, precision=highest)]
    pallas_call x0 -> x5, Pallas kernels: none -> 73.9 us  [the longest x2 43 us: gather(): pl.pallas_call(functools.partial(kernel, members), grid=(fills + members...]
    gather x1 -> x0, local copies, waits for them, and re-layouts: 54.3 us -> none  [shards(): picked = jnp.take(extended, local_index, axis=0)]
    all_to_all x0 -> x2, starting transfers between devices: none -> 25.4 us  [the longest x1 15.2 us: shards(): lax.all_to_all(partial_sums.reshape(row_count, shard, LANES), 'row', spli...]
    unnamed x25 -> x17, local copies, waits for them, and re-layouts: 19.7 us -> 1.96 us
    all_to_all x2 -> x0, local copies, waits for them, and re-layouts: 14 us -> none  [shards(): lax.all_to_all(scaled, 'mode', split_axis=1, concat_axis=2, tiled=True)]
    all_to_all x1 -> x0, blocking collectives: 10.4 us -> none  [shards(): lax.all_to_all(scaled, 'mode', split_axis=1, concat_axis=2, tiled=True)]
  transfers between devices with their start and end apart: 5 -> 6, of which waited for: 5 -> 3; matrix products, arithmetic and copies ran while one was open for 2% -> 7% of each run, Pallas kernels for 0% -> 42%
where the time goes in v1:
time: 124 us
  Pallas kernels  73.9 us (60%)
  starting transfers between devices  29.6 us (24%)
  waiting for transfers between devices  8.71 us (7%)
  other arithmetic  5.85 us (5%)
  local copies, waits for them, and re-layouts  5.04 us (4%)
    pallas_call x2, Pallas kernels, gather(): pl.pallas_call(functools.partial(kernel, members), grid=(fills + members...  43 us
    pallas_call x1, Pallas kernels, finish(): pl.pallas_call(finish_kernel, grid=(1 + steps,), in_specs=[pl.BlockSpec(m...  19.1 us
    all_to_all x1, starting transfers between devices, shards(): lax.all_to_all(partial_sums.reshape(row_count, shard, LANES), 'row', spli...  15.2 us
    all_to_all x1, starting transfers between devices, shards(): lax.all_to_all(jnp.broadcast_to(summed[None], (row_count, shard, LANES)),...  10.2 us
    pallas_call x1, Pallas kernels, project(): pl.pallas_call(project_kernel, grid=(rows // chunk,), in_specs=[pl.BlockS...  9.58 us
    ppermute x1, waiting for transfers between devices, shards(): halo = lax.ppermute(top, 'row', [(i + 1, i) for i in range(row_count - 1)])  4.41 us
    convert_element_type x1, other arithmetic, correlation(): return (numerator / denominator).astype(bf16)  4.28 us
    ppermute x1, waiting for transfers between devices, shards(): end = lax.ppermute(jnp.concatenate([halo, amp_rows], axis=0), 'mode', swap)  2.76 us
  transfers between devices with their start and end apart: 6, of which 3 were waited for; matrix products, arithmetic and copies ran while one was open for 7% of the time, Pallas kernels for 42%

profile of v1, /device:TPU:1, one launch (start us, length us, event | category | flops | bytes accessed | tf_op | source)
XLA Modules:
  0.0 124.0 jit_solution(5937069327744460402)
XLA Ops:
  0.7 2.3 %top_rows.1 = bf16[512,512]{1,0:T(8,128)(2,1)} custom-call(s32[1]{0:T(128)} %bitcast.core_ref, f32[2048,512]{1,0:T(8,128)} %vec_ref.7, f32[4,2048,256]{2,1,0:T(8,128)} %refl_ref.4), custom_call_target="tpu_custom_call" | custom-call | tf_op jit(solution)/shard_map/top_rows/pallas_call | solution.py:103
  2.9 1.4 %collective-permute-start = (bf16[512,512]{1,0:T(8,128)(2,1)}, bf16[512,512]{1,0:T(8,128)(2,1)S(1)}, u32[]{:S(2)}, u32[]{:S(2)}) collective-permute-start(bf16[512,512]{1,0:T(8,128)(2,1)} %top_rows.1), channel_id=1, source_target_pairs={{2,0},{4,2},{6,4},{8,6},{10,8},{12,10},{14,12},{16,14},{18,16},{20... | collective-permute-start | bytes 1572872 | tf_op jit(solution)/shard_map/ppermute | solution.py:421
  4.3 9.6 %project.1 = (bf16[5632,128]{1,0:T(8,128)(2,1)}, bf16[2048,512]{1,0:T(8,128)(2,1)}) custom-call(s32[1]{0:T(128)} %bitcast.core_ref, f32[4,2048,256]{2,1,0:T(8,128)} %refl_ref.4, f32[2048,512]{1,0:T(8,128)} %vec_ref.7), custom_call_target="tpu_custom_call" | custom-call | flops 4294967296 | bytes 14680064 | tf_op jit(solution)/shard_map/project/pallas_call | solution.py:72
  13.9 4.4 %collective-permute-done.halo_ref = bf16[512,512]{1,0:T(8,128)(2,1)S(1)} collective-permute-done((bf16[512,512]{1,0:T(8,128)(2,1)}, bf16[512,512]{1,0:T(8,128)(2,1)S(1)}, u32[]{:S(2)}, u32[]{:S(2)}) %collective-permute-start) | collective-permute-done | bytes 524320 | tf_op jit(solution)/shard_map/ppermute | solution.py:421
  18.3 15.2 %all-to-all-start = ((bf16[64,88,128]{2,1,0:T(8,128)(2,1)}), bf16[64,88,128]{2,1,0:T(8,128)(2,1)S(1)}, u32[]{:S(2)}, u32[]{:S(2)}) async-start(bf16[64,88,128]{2,1,0:T(8,128)(2,1)} %bitcast.9), calls=%async_computation | async-start | bytes 2883584 | tf_op jit(solution)/shard_map/all_to_all | solution.py:426
  33.5 1.9 %collective-permute-start.2 = (bf16[2048,512]{1,0:T(8,128)(2,1)}, bf16[2048,512]{1,0:T(8,128)(2,1)}, u32[]{:S(2)}, u32[]{:S(2)}) collective-permute-start(bf16[2048,512]{1,0:T(8,128)(2,1)} %get-tuple-element.31), channel_id=1, source_target_pairs={{0,1},{1,0},{2,3},{3,2},{4,5},{5,4},{6,7},{7,6},{8,9},{9,8},{10,11... | collective-permute-start | bytes 6291464 | tf_op jit(solution)/shard_map/ppermute | solution.py:430
  35.5 0.3 concatenate.6
  35.9 0.6 reshape.32.index_ref
  36.6 0.6 reshape.33.stiff_ref
  37.2 2.8 %collective-permute-done.1.end_ref = bf16[528,512]{1,0:T(8,128)(2,1)S(1)} collective-permute-done((bf16[528,512]{1,0:T(8,128)(2,1)S(1)}, bf16[528,512]{1,0:T(8,128)(2,1)S(1)}, u32[]{:S(2)}, u32[]{:S(2)}) %collective-permute-start.1) | collective-permute-done | bytes 540704 | tf_op jit(solution)/shard_map/ppermute | solution.py:438
  40.0 0.8 copy-done.2
  40.8 22.1 %gather_reflectors.1 = (bf16[4,512,1024]{2,1,0:T(8,128)(2,1)}, bf16[2048,1024]{1,0:T(8,128)(2,1)}) custom-call(s32[1]{0:T(128)} %bitcast.core_ref, s32[6144]{0:T(1024)} %reshape.32.index_ref, f32[48,512]{1,0:T(8,128)} %reshape.33.stiff_ref, f32[4,2048,256]{2,1,0:T(8,128)} %refl_ref.4, bf16[512,512]{1,0:T(8,128)(2,1)} %copy-done.1, bf16[528,512]{1,0:T(8,128)(2,1)} %copy-done.2), custom_call_target="tpu_custom_call" | custom-call | flops 1048576 | bytes 1048576 | tf_op jit(solution)/shard_map/gather_reflectors/pallas_call | solution.py:225
  62.9 0.2 reduce_sum.21
  63.1 1.3 %broadcast_in_dim.28 = bf16[64,88,128]{2,1,0:T(8,128)(2,1)} broadcast(bf16[88,128]{1,0:T(8,128)(2,1)S(1)} %reduce_sum.21), dimensions={1,2} | broadcast | bytes 1464320 | tf_op jit(solution)/shard_map/broadcast_in_dim | solution.py:452
  64.4 10.2 %all-to-all-start.1 = ((bf16[64,88,128]{2,1,0:T(8,128)(2,1)}), bf16[64,88,128]{2,1,0:T(8,128)(2,1)S(1)}, u32[]{:S(2)}, u32[]{:S(2)}) async-start(bf16[64,88,128]{2,1,0:T(8,128)(2,1)} %broadcast_in_dim.28), calls=%async_computation.1 | async-start | bytes 2883584 | tf_op jit(solution)/shard_map/all_to_all | solution.py:451
  74.7 0.1 rev.3
  74.9 4.3 %divide_convert_fusion.weight_ref = bf16[1024,1024]{1,0:T(8,128)(2,1)} fusion(f32[1024]{0:T(1024)S(1)} %bitcast.12), kind=kLoop, calls=%fused_computation | loop fusion | flops 14680064 | bytes 2101248 | tf_op jit(solution)/shard_map/convert_element_type | solution.py:399
  79.1 21.0 %gather_vectors.1.force_ref = f32[4,512,1024]{2,1,0:T(8,128)} custom-call(s32[1]{0:T(128)} %bitcast.core_ref, s32[6144]{0:T(1024)} %reshape.32.index_ref, f32[48,512]{1,0:T(8,128)} %reshape.33.stiff_ref, f32[2048,512]{1,0:T(8,128)} %vec_ref.7, bf16[2048,512]{1,0:T(8,128)(2,1)} %collective-permute-done.2.other_ref, bf16[512,512]{1,0:T(8,128)(2,1)} %copy-done.1, ...), custom_call_target="tpu_custom_call" | custom-call | flops 1048576 | bytes 1048576 | tf_op jit(solution)/shard_map/gather_vectors/pallas_call | solution.py:225
  100.1 0.7 collective-permute-start.3
  100.9 0.7 convert_reduce_fusion
  101.6 0.6 pad_maximum_fusion
  102.2 1.5 %collective-permute-done.3.other_ref = bf16[5632,128]{1,0:T(8,128)(2,1)S(1)} collective-permute-done((bf16[5632,128]{1,0:T(8,128)(2,1)S(1)}, bf16[5632,128]{1,0:T(8,128)(2,1)S(1)}, u32[]{:S(2)}, u32[]{:S(2)}) %collective-permute-start.3) | collective-permute-done | bytes 1441824 | tf_op jit(solution)/shard_map/ppermute | solution.py:462
  103.7 1.1 copy-done.7
  104.8 19.1 %finish.1 = (f32[2048,512]{1,0:T(8,128)}, f32[4,512]{1,0:T(4,128)}, f32[1,512]{1,0:T(1,128)}) custom-call(s32[1]{0:T(128)} %bitcast.core_ref, bf16[5632,128]{1,0:T(8,128)(2,1)} %bitcast.11, bf16[5632,128]{1,0:T(8,128)(2,1)} %copy-done.7, f32[4,256,256]{2,1,0:T(8,128)} %factor_ref.1, f32[2048,512]{1,0:T(8,128)} %vec_ref.7, ...), custom_call_target="tpu_custom_call" | custom-call | flops 12884901888 | bytes 31457280 | tf_op jit(solution)/shard_map/finish/pallas_call | solution.py:358
  (29 shorter events, 0.2 us)
Async XLA Ops:
  0.6 35.9 %copy-start = (f32[4,12,1024]{2,0,1:T(4,128)S(1)}, f32[4,12,1024]{2,0,1:T(4,128)}, u32[]{:S(2)}) copy-start(f32[4,12,1024]{2,0,1:T(4,128)} %param.13) | copy-start | bytes 589828
  2.9 32.5 %copy-start.5 = (f32[512]{0:T(512)S(1)}, f32[512]{0:T(512)}, u32[]{:S(2)}) copy-start(f32[512]{0:T(512)} %param.15) | copy-start | bytes 6148
  2.9 33.0 %copy-start.4 = (s32[12,1024]{1,0:T(8,128)S(1)}, s32[12,1024]{1,0:T(8,128)}, u32[]{:S(2)}) copy-start(s32[12,1024]{1,0:T(8,128)} %param.12) | copy-start | bytes 147460
  2.9 15.4 %collective-permute-start = (bf16[512,512]{1,0:T(8,128)(2,1)}, bf16[512,512]{1,0:T(8,128)(2,1)S(1)}, u32[]{:S(2)}, u32[]{:S(2)}) collective-permute-start(bf16[512,512]{1,0:T(8,128)(2,1)} %top_rows.1), channel_id=1, source_target_pairs={{2,0},{4,2},{6,4},{8,6},{10,8},{12,10},{14,12},{16,14},{18,16},{20... | collective-permute-start | bytes 1572872 | tf_op jit(solution)/shard_map/ppermute | solution.py:421
  18.3 21.7 %copy-start.1 = (bf16[512,512]{1,0:T(8,128)(2,1)}, bf16[512,512]{1,0:T(8,128)(2,1)S(1)}, u32[]{:S(2)}) copy-start(bf16[512,512]{1,0:T(8,128)(2,1)S(1)} %collective-permute-done.halo_ref) | copy-start | bytes 1572868
  18.3 44.5 %all-to-all-start = ((bf16[64,88,128]{2,1,0:T(8,128)(2,1)}), bf16[64,88,128]{2,1,0:T(8,128)(2,1)S(1)}, u32[]{:S(2)}, u32[]{:S(2)}) async-start(bf16[64,88,128]{2,1,0:T(8,128)(2,1)} %bitcast.9), calls=%async_computation | async-start | bytes 2883584 | tf_op jit(solution)/shard_map/all_to_all | solution.py:426
  33.5 45.6 %collective-permute-start.2 = (bf16[2048,512]{1,0:T(8,128)(2,1)}, bf16[2048,512]{1,0:T(8,128)(2,1)}, u32[]{:S(2)}, u32[]{:S(2)}) collective-permute-start(bf16[2048,512]{1,0:T(8,128)(2,1)} %get-tuple-element.31), channel_id=1, source_target_pairs={{0,1},{1,0},{2,3},{3,2},{4,5},{5,4},{6,7},{7,6},{8,9},{9,8},{10,11... | collective-permute-start | bytes 6291464 | tf_op jit(solution)/shard_map/ppermute | solution.py:430
  35.8 4.2 %collective-permute-start.1 = (bf16[528,512]{1,0:T(8,128)(2,1)S(1)}, bf16[528,512]{1,0:T(8,128)(2,1)S(1)}, u32[]{:S(2)}, u32[]{:S(2)}) collective-permute-start(bf16[528,512]{1,0:T(8,128)(2,1)S(1)} %concatenate.6), channel_id=1, source_target_pairs={{0,1},{1,0},{2,3},{3,2},{4,5},{5,4},{6,7},{7,6},{8,9},{9,8},{10,11... | collective-permute-start | bytes 1622024 | tf_op jit(solution)/shard_map/ppermute | solution.py:438
  40.0 0.8 copy-start.2
  62.9 11.8 %copy-start.6 = (f32[1024]{0:T(1024)S(1)}, f32[1024]{0:T(1024)}, u32[]{:S(2)}) copy-start(f32[1024]{0:T(1024)} %param.14) | copy-start | bytes 12292
  64.4 35.7 %all-to-all-start.1 = ((bf16[64,88,128]{2,1,0:T(8,128)(2,1)}), bf16[64,88,128]{2,1,0:T(8,128)(2,1)S(1)}, u32[]{:S(2)}, u32[]{:S(2)}) async-start(bf16[64,88,128]{2,1,0:T(8,128)(2,1)} %broadcast_in_dim.28), calls=%async_computation.1 | async-start | bytes 2883584 | tf_op jit(solution)/shard_map/all_to_all | solution.py:451
  100.1 3.6 %copy-start.3 = (bf16[64,88,128]{2,1,0:T(8,128)(2,1)}, bf16[64,88,128]{2,1,0:T(8,128)(2,1)S(1)}, u32[]{:S(2)}) copy-start(bf16[64,88,128]{2,1,0:T(8,128)(2,1)S(1)} %all-to-all-done.1) | copy-start | bytes 4325380
  100.1 3.6 %collective-permute-start.3 = (bf16[5632,128]{1,0:T(8,128)(2,1)S(1)}, bf16[5632,128]{1,0:T(8,128)(2,1)S(1)}, u32[]{:S(2)}, u32[]{:S(2)}) collective-permute-start(bf16[5632,128]{1,0:T(8,128)(2,1)S(1)} %bitcast.10), channel_id=1, source_target_pairs={{0,1},{1,0},{2,3},{3,2},{4,5},{5,4},{6,7},{7,6},{8,9},{9,8},{10,11... | collective-permute-start | bytes 4325384 | tf_op jit(solution)/shard_map/ppermute | solution.py:462
  103.7 1.1 copy-start.7

commit v2 on v1

--- a/solution.py
+++ b/solution.py
@@ -16,7 +16,7 @@
 LANES = 128
 bf16 = jnp.bfloat16
 f32 = jnp.float32
-VMEM_LIMIT = 58 * 1024 * 1024
+MIB = 1024 * 1024
 
 damping_ratio = 0.05
 PAIRS = (((0, 3), (1, 3), (2, 3)), ((0, 2), (1, 2), (0, 1)))
@@ -86,7 +86,7 @@
             jax.ShapeDtypeStruct((rows, cols), bf16),
         ],
         scratch_shapes=[pltpu.VMEM((cols, PANELS * COLS), f32), pltpu.VMEM((COLS, 3 * COLS), f32)],
-        compiler_params=pltpu.CompilerParams(vmem_limit_bytes=VMEM_LIMIT),
+        compiler_params=pltpu.CompilerParams(vmem_limit_bytes=58 * MIB),
         cost_estimate=pl.CostEstimate(flops=4 * rows * 256 * 512 * 4, bytes_accessed=14 << 20, transcendentals=0),
         name="project",
     )(core, reflectors, vectors)
@@ -110,6 +110,7 @@
         ],
         out_specs=pl.BlockSpec((2 * HALO, cols), lambda i: (0, 0)),
         out_shape=jax.ShapeDtypeStruct((2 * HALO, cols), bf16),
+        compiler_params=pltpu.CompilerParams(vmem_limit_bytes=58 * MIB),
         name="top_rows",
     )(core, vectors, reflectors)
 
@@ -128,26 +129,31 @@
     return slice(s * LANES, (s + 1) * LANES)
 
 
-def spread_coefs(stiff_ref, wide):
-    stiff = stiff_ref[...]
+def spread_coefs(stiff_ref, wide, group):
+    stiff = stiff_ref[:, pl.ds(pl.multiple_of(group * GROUP, GROUP), GROUP)]
+    base = group * GROUP * TERMS
     high = stiff.astype(bf16)
     low = (stiff - high.astype(f32)).astype(bf16)
     both = jnp.concatenate([high, low], axis=1)
-    lane = lax.broadcasted_iota(jnp.int32, (1, 2 * GROUP), 1) % GROUP
-    ones = jnp.ones((2 * GROUP, LANES), bf16)
-    for start in range(0, GROUP, AT_ONCE):
+    pair = lax.broadcasted_iota(jnp.int32, (1, 2 * GROUP), 1) % GROUP // 2
+    odd = lax.broadcasted_iota(jnp.int32, (2 * GROUP, 2 * LANES), 0) % 2
+    right = lax.broadcasted_iota(jnp.int32, (2 * GROUP, 2 * LANES), 1) // LANES
+    select = jnp.where(odd == right, 1.0, 0.0).astype(bf16)
+    for start in range(0, GROUP // 2, AT_ONCE):
         picked = [
-            both * jnp.where(lane == e, 1.0, 0.0).astype(bf16) for e in range(start, start + AT_ONCE)
+            both * jnp.where(pair == e, 1.0, 0.0).astype(bf16) for e in range(start, start + AT_ONCE)
         ]
-        wide[start * TERMS : (start + AT_ONCE) * TERMS] = mm(jnp.concatenate(picked, axis=0), ones)
-
-
-def member_rows(index_ref, stiff_ref, table, wide, sums, out_ref, step, members):
-    spread_coefs(stiff_ref, wide)
-
+        spread = mm(jnp.concatenate(picked, axis=0), select)
+        for t in range(AT_ONCE):
+            for h in range(2):
+                at = (2 * (start + t) + h) * TERMS
+                wide[pl.ds(pl.multiple_of(base + at, 8), TERMS), :] = spread[t * TERMS : (t + 1) * TERMS, strip(h)]
+
+
+def member_rows(index_ref, table, wide, sums, out_ref, step, members):
     def one(i, _):
         e = step * GROUP + i
-        stiff = wide[pl.ds(pl.multiple_of(i * TERMS, 8), TERMS), :]
+        stiff = wide[pl.ds(pl.multiple_of(e * TERMS, 8), TERMS), :]
         acc = [None] * COMPS
         for k in range(MEM_DOFS):
             at = pl.multiple_of(index_ref[k * members + e], 8)
@@ -173,6 +179,9 @@
 
     @pl.when(step < fills)
     def _():
+        share = members // GROUP // fills
+        for g in range(share):
+            spread_coefs(stiff_ref, wide, step * share + g)
         for s in range(8):
             lay_out(table, step * FILL, s, refl_ref[s // 2, :, strip(s % 2)])
         for p in range(PANELS):
@@ -187,7 +196,7 @@
 
     @pl.when(step >= fills)
     def _():
-        member_rows(index_ref, stiff_ref, table, wide, sums, out_ref, step - fills, members)
+        member_rows(index_ref, table, wide, sums, out_ref, step - fills, members)
 
 
 def vec_kernel(members, core_ref, index_ref, stiff_ref, vec_ref, other_ref, halo_ref, end_ref, out_ref, table, wide, sums):
@@ -197,6 +206,9 @@
 
     @pl.when(step < fills)
     def _():
+        share = members // GROUP // fills
+        for g in range(share):
+            spread_coefs(stiff_ref, wide, step * share + g)
         for s in range(4):
             lay_out(table, step * FILL, s, vec_ref[:, strip(s)])
             lay_out(table, step * FILL, 4 + s, other_ref[:, strip(s)])
@@ -209,7 +221,7 @@
 
     @pl.when(step >= fills)
     def _():
-        member_rows(index_ref, stiff_ref, table, wide, sums, out_ref, step - fills, members)
+        member_rows(index_ref, table, wide, sums, out_ref, step - fills, members)
 
 
 def gather(kernel, name, rows, core, index, stiff, blocks, block_specs, out_shape, flat=False):
@@ -225,17 +237,17 @@
     return pl.pallas_call(
         functools.partial(kernel, members),
         grid=(fills + members // GROUP,),
-        in_specs=[smem, smem, pl.BlockSpec((TERMS, GROUP), lambda i: (0, group_at(i)))]
+        in_specs=[smem, smem, pl.BlockSpec((TERMS, members), whole)]
         + [spec(fill_at) for spec in block_specs]
         + [pl.BlockSpec((2 * HALO, MODES // 2), whole), pl.BlockSpec((2 * HALO + 16, MODES // 2), whole)],
         out_specs=out_specs,
         out_shape=out_shape,
         scratch_shapes=[
             pltpu.VMEM(((rows + HALO) * 8, LANES), f32),
-            pltpu.VMEM((TERMS * GROUP, LANES), f32),
+            pltpu.VMEM((TERMS * members, LANES), f32),
             pltpu.VMEM((COMPS * GROUP * 8, LANES), f32),
         ],
-        compiler_params=pltpu.CompilerParams(vmem_limit_bytes=VMEM_LIMIT),
+        compiler_params=pltpu.CompilerParams(vmem_limit_bytes=58 * MIB),
         cost_estimate=pl.CostEstimate(flops=1 << 20, bytes_accessed=1 << 20, transcendentals=0),
         name=name,
     )(core, index, stiff, *blocks)
@@ -309,22 +321,48 @@
 
 
 def finish_kernel(
-    core_ref, mine_ref, other_ref, factor_ref, vec_ref, flat_ref, force_ref, refl_ref, weight_ref, amp_ref,
-    cap_ref, ratio_ref, out_ref, demand_ref, resized_ref, coef,
+    steps, core_ref, mine_ref, other_ref, factor_ref, vec_hbm, flat_hbm, force_hbm, refl_hbm, weight_hbm, amp_ref,
+    cap_ref, ratio_ref, out_hbm, demand_ref, resized_ref, coef, vec_buf, flat_buf, force_buf, refl_buf, weight_ref,
+    out_buf, in_sems, out_sems, weight_sem,
 ):
-    step = pl.program_id(0)
+    chunk = vec_buf.shape[1]
+    group = force_buf.shape[2]
+
+    def copies(i):
+        slot = i % 2
+        rows = pl.ds(i * chunk, chunk)
+        found = pl.ds(i * group, group)
+        return [
+            pltpu.make_async_copy(refl_hbm.at[:, found], refl_buf.at[slot], in_sems.at[slot, 0]),
+            pltpu.make_async_copy(force_hbm.at[:, found], force_buf.at[slot], in_sems.at[slot, 1]),
+            pltpu.make_async_copy(flat_hbm.at[rows], flat_buf.at[slot], in_sems.at[slot, 2]),
+            pltpu.make_async_copy(vec_hbm.at[rows], vec_buf.at[slot], in_sems.at[slot, 3]),
+        ]
+
+    weight_copy = pltpu.make_async_copy(weight_hbm, weight_ref, weight_sem)
+    for i in range(2):
+        for copy in copies(i):
+            copy.start()
+        if i == 0:
+            weight_copy.start()
+
     for core in range(2):
 
-        @pl.when((step == 0) & (core_ref[0] == core))
+        @pl.when(core_ref[0] == core)
         def _():
             pair = (mine_ref, other_ref) if core == 0 else (other_ref, mine_ref)
             solve_panels(*pair, mine_ref, other_ref, factor_ref, coef)
 
-    @pl.when(step > 0)
-    def _():
-        group = force_ref.shape[1]
-        force = force_ref[...].reshape(COMPS * group, MODES)
-        force = force - mm(refl_ref[...].reshape(COMPS * group, MODES), coef[...])
+    out_copies = []
+    for i in range(steps):
+        slot = i % 2
+        refl_copy, force_copy, flat_copy, vec_copy = copies(i)
+        refl_copy.wait()
+        force_copy.wait()
+        if i == 0:
+            weight_copy.wait()
+        force = force_buf[slot].reshape(COMPS * group, MODES)
+        force = force - mm(refl_buf[slot].reshape(COMPS * group, MODES), coef[...])
         scaled = (force * amp_ref[...]).astype(bf16)
         part = None
         for b in range(MODES // COLS):
@@ -333,18 +371,31 @@
             weighted = mm(scaled[:, here], weight_ref[here, here])
             if b > 0:
                 weighted = weighted + 2.0 * mm(scaled[:, : b * COLS], weight_ref[: b * COLS, here])
-            product = weighted * scaled[:, b * COLS : upto].astype(f32)
+            product = weighted * scaled[:, here].astype(f32)
             both = product[:, :LANES] + product[:, LANES:]
             part = both if part is None else part + both
+        along = slice(i * group, (i + 1) * group)
         total = jnp.full((1, group), 0.25, f32)
         for c in range(COMPS):
             combined = jnp.sum(part[c * group : (c + 1) * group].T, axis=0, keepdims=True)
-            capacity = cap_ref[c : c + 1]
+            capacity = cap_ref[c : c + 1, along]
             demand = combined / (capacity * capacity)
-            demand_ref[c : c + 1] = demand
+            demand_ref[c : c + 1, along] = demand
             total = total + demand
-        resized_ref[...] = ratio_ref[...] * jnp.sqrt(total)
-        out_ref[...] = vec_ref[...] - mm(flat_ref[...], coef[:, : out_ref.shape[1]])
+        resized_ref[:, along] = ratio_ref[:, along] * jnp.sqrt(total)
+        flat_copy.wait()
+        vec_copy.wait()
+        if i >= 2:
+            out_copies[i - 2].wait()
+        out_buf[slot] = vec_buf[slot] - mm(flat_buf[slot], coef[:, : out_buf.shape[2]])
+        out_copy = pltpu.make_async_copy(out_buf.at[slot], out_hbm.at[pl.ds(i * chunk, chunk)], out_sems.at[slot])
+        out_copy.start()
+        out_copies.append(out_copy)
+        if i + 2 < steps:
+            for copy in copies(i + 2):
+                copy.start()
+    for out_copy in out_copies[-2:]:
+        out_copy.wait()
 
 
 def finish(core, mine, other, factors, vectors, flat, from_vec, from_refl, weights, amp, capacity, ratio):
@@ -353,49 +404,48 @@
     group = 128
     steps = members // group
     chunk = rows // steps
-    whole = pl.BlockSpec(memory_space=pltpu.VMEM)
-    at = lambda i: jnp.maximum(i - 1, 0)
+    here = pl.BlockSpec(memory_space=pltpu.VMEM)
+    there = pl.BlockSpec(memory_space=pl.ANY)
     return pl.pallas_call(
-        finish_kernel,
-        grid=(1 + steps,),
-        in_specs=[
-            pl.BlockSpec(memory_space=pltpu.SMEM),
-            whole,
-            whole,
-            whole,
-            pl.BlockSpec((chunk, cols), lambda i: (at(i), 0)),
-            pl.BlockSpec((chunk, MODES), lambda i: (at(i), 0)),
-            pl.BlockSpec((COMPS, group, MODES), lambda i: (0, at(i), 0)),
-            pl.BlockSpec((COMPS, group, MODES), lambda i: (0, at(i), 0)),
-            whole,
-            whole,
-            pl.BlockSpec((COMPS, group), lambda i: (0, at(i))),
-            pl.BlockSpec((1, group), lambda i: (0, at(i))),
-        ],
-        out_specs=[
-            pl.BlockSpec((chunk, cols), lambda i: (at(i), 0)),
-            pl.BlockSpec((COMPS, group), lambda i: (0, at(i))),
-            pl.BlockSpec((1, group), lambda i: (0, at(i))),
-        ],
+        functools.partial(finish_kernel, steps),
+        in_specs=[pl.BlockSpec(memory_space=pltpu.SMEM), here, here, here]
+        + [there] * 5
+        + [here] * 3,
+        out_specs=[there, here, here],
         out_shape=[
             jax.ShapeDtypeStruct((rows, cols), f32),
             jax.ShapeDtypeStruct((COMPS, members), f32),
             jax.ShapeDtypeStruct((1, members), f32),
         ],
-        scratch_shapes=[pltpu.VMEM((PANELS * COLS, MODES), bf16)],
-        compiler_params=pltpu.CompilerParams(vmem_limit_bytes=VMEM_LIMIT),
+        scratch_shapes=[
+            pltpu.VMEM((PANELS * COLS, MODES), bf16),
+            pltpu.VMEM((2, chunk, cols), f32),
+            pltpu.VMEM((2, chunk, MODES), bf16),
+            pltpu.VMEM((2, COMPS, group, MODES), f32),
+            pltpu.VMEM((2, COMPS, group, MODES), bf16),
+            pltpu.VMEM((MODES, MODES), bf16),
+            pltpu.VMEM((2, chunk, cols), f32),
+            pltpu.SemaphoreType.DMA((2, 4)),
+            pltpu.SemaphoreType.DMA((2,)),
+            pltpu.SemaphoreType.DMA,
+        ],
+        compiler_params=pltpu.CompilerParams(vmem_limit_bytes=58 * MIB),
         cost_estimate=pl.CostEstimate(flops=12 << 30, bytes_accessed=30 << 20, transcendentals=0),
         name="finish",
     )(core, mine, other, factors, vectors, flat, from_vec, from_refl, weights, amp, capacity, ratio)
 
 
 def correlation(frequency):
-    freq_ratio = frequency[None, :] / frequency[:, None]
+    inverse = 1.0 / frequency
+    root = jnp.sqrt(frequency)
+    inverse_root = 1.0 / root
     squared = damping_ratio * damping_ratio
-    numerator = 8.0 * squared * (1.0 + freq_ratio) * freq_ratio * jnp.sqrt(freq_ratio)
-    denominator = (1.0 - freq_ratio * freq_ratio) ** 2 + 4.0 * squared * freq_ratio * (
-        1.0 + freq_ratio
-    ) ** 2
+    ratio = frequency[None, :] * inverse[:, None]
+    power = (frequency * root)[None, :] * (inverse * inverse_root)[:, None]
+    above = 1.0 + ratio
+    below = 1.0 - ratio
+    numerator = (8.0 * squared) * above * power
+    denominator = (above * above) * (below * below + (4.0 * squared) * ratio)
     return (numerator / denominator).astype(bf16)
 
 
@@ -421,13 +471,17 @@
     halo = lax.ppermute(top, "row", [(i + 1, i) for i in range(row_count - 1)])
     _, reflectors_after = lax.optimization_barrier((top, reflectors))
     partial_sums, half = project(core_arr, reflectors_after, eigenvectors)
-    partial_sums, halo = lax.optimization_barrier((partial_sums, halo))
+    first_row = lax.axis_index("row") * rows
+    index = lax.dynamic_slice_in_dim(dof_index, core * members, members, axis=1)
+    index = ((index - first_row) * 8).reshape(-1)
+    stiff = lax.dynamic_slice_in_dim(stiffness, core * members, members, axis=2)
+    stiff = stiff.reshape(TERMS, members)
+    partial_sums, halo, index, stiff = lax.optimization_barrier((partial_sums, halo, index, stiff))
     shard = partial_sums.shape[0] // row_count
     pieces = lax.all_to_all(
         partial_sums.reshape(row_count, shard, LANES), "row", split_axis=0, concat_axis=0, tiled=True
     )
 
-    other = lax.ppermute(half, "mode", swap)
     amp_high = amplitude.astype(bf16)
     amp_rest = amplitude - amp_high.astype(f32)
     amp_mid = amp_rest.astype(bf16)
@@ -436,14 +490,11 @@
         [amp_high[None], amp_mid[None], amp_low[None], jnp.zeros((13, cols), bf16)], axis=0
     )
     end = lax.ppermute(jnp.concatenate([halo, amp_rows], axis=0), "mode", swap)
+    end, half = lax.optimization_barrier((end, half))
+    other = lax.ppermute(half, "mode", swap)
     amp_other = jnp.sum(end[2 * HALO : 2 * HALO + 3].astype(f32), axis=0)
     amp_all = jnp.concatenate([amplitude, amp_other])[None]
 
-    first_row = lax.axis_index("row") * rows
-    index = lax.dynamic_slice_in_dim(dof_index, core * members, members, axis=1)
-    index = ((index - first_row) * 8).reshape(-1)
-    stiff = lax.dynamic_slice_in_dim(stiffness, core * members, members, axis=2)
-    stiff = stiff.reshape(TERMS, members)
     from_refl, flat = gather_reflectors(core_arr, index, stiff, reflectors, halo, end)
     pieces, from_refl, flat = lax.optimization_barrier((pieces, from_refl, flat))
     summed = jnp.sum(pieces.astype(f32), axis=0).astype(bf16)

time: 124 us -> 118 us (0.952)
  Pallas kernels: 73.9 us -> 69.5 us
  waiting for transfers between devices: 8.71 us -> 6.67 us
    pallas_call x2, Pallas kernels: 43 us -> 38.5 us  [gather(): pl.pallas_call(functools.partial(kernel, members), grid=(fills + members...]
    ppermute x1, starting transfers between devices: 0.12 us -> 1.91 us  [shards(): end = lax.ppermute(jnp.concatenate([halo, amp_rows], axis=0), 'mode', swap)]
    ppermute x1, starting transfers between devices: 1.91 us -> 0.37 us  [shards(): other = lax.ppermute(half, 'mode', swap)]
    ppermute x1, waiting for transfers between devices: 4.41 us -> 3.07 us  [shards(): halo = lax.ppermute(top, 'row', [(i + 1, i) for i in range(row_count - 1)])]
  transfers between devices with their start and end apart: 6 -> 6, of which waited for: 3 -> 4; matrix products, arithmetic and copies ran while one was open for 7% -> 7% of each run, Pallas kernels for 42% -> 41%
where the time goes in v2:
time: 118 us; the launch traced here: 117 us
  Pallas kernels  69.5 us (59%)
  starting transfers between devices  30.6 us (26%)
  waiting for transfers between devices  6.67 us (6%)
  other arithmetic  4.7 us (4%)
  local copies, waits for them, and re-layouts  4.68 us (4%)
    pallas_call x2, Pallas kernels, gather(): pl.pallas_call(functools.partial(kernel, members), grid=(fills + members...  38.5 us
    pallas_call x1, Pallas kernels, finish(): pl.pallas_call(functools.partial(finish_kernel, steps), in_specs=[pl.Bloc...  19.1 us
    all_to_all x1, starting transfers between devices, shards(): lax.all_to_all(partial_sums.reshape(row_count, shard, LANES), 'row', spli...  15.2 us
    all_to_all x1, starting transfers between devices, shards(): lax.all_to_all(jnp.broadcast_to(summed[None], (row_count, shard, LANES)),...  10 us
    pallas_call x1, Pallas kernels, project(): pl.pallas_call(project_kernel, grid=(rows // chunk,), in_specs=[pl.BlockS...  9.57 us
    convert_element_type x1, other arithmetic, correlation(): return (numerator / denominator).astype(bf16)  3.11 us
    ppermute x1, waiting for transfers between devices, shards(): halo = lax.ppermute(top, 'row', [(i + 1, i) for i in range(row_count - 1)])  3.07 us
  transfers between devices with their start and end apart: 6, of which 4 were waited for; matrix products, arithmetic and copies ran while one was open for 7% of the time, Pallas kernels for 41%

profile of v2, /device:TPU:1, one launch (start us, length us, event | category | flops | bytes accessed | tf_op | source)
XLA Modules:
  0.0 117.1 jit_solution(7265837558832847807)
XLA Ops:
  0.7 2.3 %top_rows.1 = bf16[512,512]{1,0:T(8,128)(2,1)} custom-call(s32[1]{0:T(128)} %bitcast.core_ref, f32[2048,512]{1,0:T(8,128)} %vec_hbm.1, f32[4,2048,256]{2,1,0:T(8,128)} %refl_ref.4), custom_call_target="tpu_custom_call" | custom-call | tf_op jit(solution)/shard_map/top_rows/pallas_call | solution.py:103
  2.9 1.3 %collective-permute-start = (bf16[512,512]{1,0:T(8,128)(2,1)}, bf16[512,512]{1,0:T(8,128)(2,1)S(1)}, u32[]{:S(2)}, u32[]{:S(2)}) collective-permute-start(bf16[512,512]{1,0:T(8,128)(2,1)} %top_rows.1), channel_id=1, source_target_pairs={{2,0},{4,2},{6,4},{8,6},{10,8},{12,10},{14,12},{16,14},{18,16},{20... | collective-permute-start | bytes 1572872 | tf_op jit(solution)/shard_map/ppermute | solution.py:471
  4.3 0.6 reshape.53.index_ref
  4.9 0.6 reshape.54.stiff_ref
  5.6 9.6 %project.1 = (bf16[5632,128]{1,0:T(8,128)(2,1)}, bf16[2048,512]{1,0:T(8,128)(2,1)}) custom-call(s32[1]{0:T(128)} %bitcast.core_ref, f32[4,2048,256]{2,1,0:T(8,128)} %refl_ref.4, f32[2048,512]{1,0:T(8,128)} %vec_hbm.1), custom_call_target="tpu_custom_call" | custom-call | flops 4294967296 | bytes 14680064 | tf_op jit(solution)/shard_map/project/pallas_call | solution.py:72
  15.2 3.1 %collective-permute-done.halo_ref = bf16[512,512]{1,0:T(8,128)(2,1)S(1)} collective-permute-done((bf16[512,512]{1,0:T(8,128)(2,1)}, bf16[512,512]{1,0:T(8,128)(2,1)S(1)}, u32[]{:S(2)}, u32[]{:S(2)}) %collective-permute-start) | collective-permute-done | bytes 524320 | tf_op jit(solution)/shard_map/ppermute | solution.py:471
  18.2 15.2 %all-to-all-start = ((bf16[64,88,128]{2,1,0:T(8,128)(2,1)}), bf16[64,88,128]{2,1,0:T(8,128)(2,1)S(1)}, u32[]{:S(2)}, u32[]{:S(2)}) async-start(bf16[64,88,128]{2,1,0:T(8,128)(2,1)} %bitcast.11), calls=%async_computation | async-start | bytes 2883584 | tf_op jit(solution)/shard_map/all_to_all | solution.py:481
  33.5 0.3 concatenate.6
  33.8 1.9 %collective-permute-start.1 = (bf16[528,512]{1,0:T(8,128)(2,1)S(1)}, bf16[528,512]{1,0:T(8,128)(2,1)S(1)}, u32[]{:S(2)}, u32[]{:S(2)}) collective-permute-start(bf16[528,512]{1,0:T(8,128)(2,1)S(1)} %concatenate.6), channel_id=1, source_target_pairs={{0,1},{1,0},{2,3},{3,2},{4,5},{5,4},{6,7},{7,6},{8,9},{9,8},{10,11... | collective-permute-start | bytes 1622024 | tf_op jit(solution)/shard_map/ppermute | solution.py:492
  35.7 1.6 %collective-permute-done.1.end_ref = bf16[528,512]{1,0:T(8,128)(2,1)S(1)} collective-permute-done((bf16[528,512]{1,0:T(8,128)(2,1)S(1)}, bf16[528,512]{1,0:T(8,128)(2,1)S(1)}, u32[]{:S(2)}, u32[]{:S(2)}) %collective-permute-start.1) | collective-permute-done | bytes 540704 | tf_op jit(solution)/shard_map/ppermute | solution.py:492
  37.3 0.4 collective-permute-start.2
  37.7 0.4 copy-done.2
  38.1 20.1 %gather_reflectors.1 = (bf16[4,512,1024]{2,1,0:T(8,128)(2,1)}, bf16[2048,1024]{1,0:T(8,128)(2,1)}) custom-call(s32[1]{0:T(128)} %bitcast.core_ref, s32[6144]{0:T(1024)} %reshape.53.index_ref, f32[48,512]{1,0:T(8,128)} %reshape.54.stiff_ref, f32[4,2048,256]{2,1,0:T(8,128)} %refl_ref.4, bf16[512,512]{1,0:T(8,128)(2,1)} %copy-done.1, bf16[528,512]{1,0:T(8,128)(2,1)} %copy-done.2), custom_call_target="tpu_custom_call" | custom-call | flops 1048576 | bytes 1048576 | tf_op jit(solution)/shard_map/gather_reflectors/pallas_call | solution.py:237
  58.4 1.3 %broadcast_in_dim.31 = bf16[64,88,128]{2,1,0:T(8,128)(2,1)} broadcast(bf16[88,128]{1,0:T(8,128)(2,1)S(1)} %reduce_sum.21), dimensions={1,2} | broadcast | bytes 1464320 | tf_op jit(solution)/shard_map/broadcast_in_dim | solution.py:503
  59.8 10.0 %all-to-all-start.1 = ((bf16[64,88,128]{2,1,0:T(8,128)(2,1)}), bf16[64,88,128]{2,1,0:T(8,128)(2,1)S(1)}, u32[]{:S(2)}, u32[]{:S(2)}) async-start(bf16[64,88,128]{2,1,0:T(8,128)(2,1)} %broadcast_in_dim.31), calls=%async_computation.1 | async-start | bytes 2883584 | tf_op jit(solution)/shard_map/all_to_all | solution.py:502
  70.0 3.1 %fusion.7.weight_hbm = bf16[1024,1024]{1,0:T(8,128)(2,1)} fusion(f32[1024]{0:T(1024)S(1)} %get-tuple-element.51, f32[1024]{0:T(1024)S(1)} %get-tuple-element.50, f32[1024]{0:T(1024)S(1)} %get-tuple-element.49, f32[1024]{0:T(1024)S(1)} %bitcast.13), kind=kLoop, calls=%fused_computation.10 | loop fusion | flops 13631488 | bytes 2113536 | tf_op jit(solution)/shard_map/convert_element_type | solution.py:449
  73.1 18.3 %gather_vectors.1.force_hbm = f32[4,512,1024]{2,1,0:T(8,128)} custom-call(s32[1]{0:T(128)} %bitcast.core_ref, s32[6144]{0:T(1024)} %reshape.53.index_ref, f32[48,512]{1,0:T(8,128)} %reshape.54.stiff_ref, f32[2048,512]{1,0:T(8,128)} %vec_hbm.1, bf16[2048,512]{1,0:T(8,128)(2,1)} %collective-permute-done.2.other_ref, bf16[512,512]{1,0:T(8,128)(2,1)} %copy-done.1, ...), custom_call_target="tpu_custom_call" | custom-call | flops 1048576 | bytes 1048576 | tf_op jit(solution)/shard_map/gather_vectors/pallas_call | solution.py:237
  91.5 0.5 all-to-all-done.1
  92.0 1.8 %collective-permute-start.3 = (bf16[5632,128]{1,0:T(8,128)(2,1)S(1)}, bf16[5632,128]{1,0:T(8,128)(2,1)S(1)}, u32[]{:S(2)}, u32[]{:S(2)}) collective-permute-start(bf16[5632,128]{1,0:T(8,128)(2,1)S(1)} %bitcast.9), channel_id=1, source_target_pairs={{0,1},{1,0},{2,3},{3,2},{4,5},{5,4},{6,7},{7,6},{8,9},{9,8},{10,11... | collective-permute-start | bytes 4325384 | tf_op jit(solution)/shard_map/ppermute | solution.py:513
  93.8 0.7 convert_reduce_fusion
  94.5 0.6 pad_maximum_fusion
  95.1 1.5 %collective-permute-done.3.other_ref = bf16[5632,128]{1,0:T(8,128)(2,1)S(1)} collective-permute-done((bf16[5632,128]{1,0:T(8,128)(2,1)S(1)}, bf16[5632,128]{1,0:T(8,128)(2,1)S(1)}, u32[]{:S(2)}, u32[]{:S(2)}) %collective-permute-start.3) | collective-permute-done | bytes 1441824 | tf_op jit(solution)/shard_map/ppermute | solution.py:513
  96.7 1.1 copy-done.7
  97.8 19.1 %finish.1 = (f32[2048,512]{1,0:T(8,128)}, f32[4,512]{1,0:T(4,128)}, f32[1,512]{1,0:T(1,128)}) custom-call(s32[1]{0:T(128)} %bitcast.core_ref, bf16[5632,128]{1,0:T(8,128)(2,1)} %bitcast.10, bf16[5632,128]{1,0:T(8,128)(2,1)} %copy-done.7, f32[4,256,256]{2,1,0:T(8,128)} %factor_ref.1, f32[2048,512]{1,0:T(8,128)} %vec_hbm.1, ...), custom_call_target="tpu_custom_call" | custom-call | flops 12884901888 | bytes 31457280 | tf_op jit(solution)/shard_map/finish/pallas_call | solution.py:409
  (30 shorter events, 0.5 us)
Async XLA Ops:
  0.6 4.3 %copy-start = (f32[4,12,1024]{2,0,1:T(4,128)S(1)}, f32[4,12,1024]{2,0,1:T(4,128)}, u32[]{:S(2)}) copy-start(f32[4,12,1024]{2,0,1:T(4,128)} %param.13) | copy-start | bytes 589828
  0.7 3.6 %copy-start.4 = (s32[12,1024]{1,0:T(8,128)S(1)}, s32[12,1024]{1,0:T(8,128)}, u32[]{:S(2)}) copy-start(s32[12,1024]{1,0:T(8,128)} %param.12) | copy-start | bytes 147460
  2.9 15.3 %collective-permute-start = (bf16[512,512]{1,0:T(8,128)(2,1)}, bf16[512,512]{1,0:T(8,128)(2,1)S(1)}, u32[]{:S(2)}, u32[]{:S(2)}) collective-permute-start(bf16[512,512]{1,0:T(8,128)(2,1)} %top_rows.1), channel_id=1, source_target_pairs={{2,0},{4,2},{6,4},{8,6},{10,8},{12,10},{14,12},{16,14},{18,16},{20... | collective-permute-start | bytes 1572872 | tf_op jit(solution)/shard_map/ppermute | solution.py:471
  5.6 27.8 %copy-start.5 = (f32[512]{0:T(512)S(1)}, f32[512]{0:T(512)}, u32[]{:S(2)}) copy-start(f32[512]{0:T(512)} %param.15) | copy-start | bytes 6148
  18.2 19.4 %copy-start.1 = (bf16[512,512]{1,0:T(8,128)(2,1)}, bf16[512,512]{1,0:T(8,128)(2,1)S(1)}, u32[]{:S(2)}) copy-start(bf16[512,512]{1,0:T(8,128)(2,1)S(1)} %collective-permute-done.halo_ref) | copy-start | bytes 1572868
  18.2 40.0 %all-to-all-start = ((bf16[64,88,128]{2,1,0:T(8,128)(2,1)}), bf16[64,88,128]{2,1,0:T(8,128)(2,1)S(1)}, u32[]{:S(2)}, u32[]{:S(2)}) async-start(bf16[64,88,128]{2,1,0:T(8,128)(2,1)} %bitcast.11), calls=%async_computation | async-start | bytes 2883584 | tf_op jit(solution)/shard_map/all_to_all | solution.py:481
  33.8 3.5 %collective-permute-start.1 = (bf16[528,512]{1,0:T(8,128)(2,1)S(1)}, bf16[528,512]{1,0:T(8,128)(2,1)S(1)}, u32[]{:S(2)}, u32[]{:S(2)}) collective-permute-start(bf16[528,512]{1,0:T(8,128)(2,1)S(1)} %concatenate.6), channel_id=1, source_target_pairs={{0,1},{1,0},{2,3},{3,2},{4,5},{5,4},{6,7},{7,6},{8,9},{9,8},{10,11... | collective-permute-start | bytes 1622024 | tf_op jit(solution)/shard_map/ppermute | solution.py:492
  37.3 0.8 copy-start.2
  37.3 35.9 %collective-permute-start.2 = (bf16[2048,512]{1,0:T(8,128)(2,1)}, bf16[2048,512]{1,0:T(8,128)(2,1)}, u32[]{:S(2)}, u32[]{:S(2)}) collective-permute-start(bf16[2048,512]{1,0:T(8,128)(2,1)} %get-tuple-element.39), channel_id=1, source_target_pairs={{0,1},{1,0},{2,3},{3,2},{4,5},{5,4},{6,7},{7,6},{8,9},{9,8},{10,11... | collective-permute-start | bytes 6291464 | tf_op jit(solution)/shard_map/ppermute | solution.py:494
  58.2 11.6 %copy-start.6 = (f32[1024]{0:T(1024)S(1)}, f32[1024]{0:T(1024)}, u32[]{:S(2)}) copy-start(f32[1024]{0:T(1024)} %param.14) | copy-start | bytes 12292
  59.8 32.2 %all-to-all-start.1 = ((bf16[64,88,128]{2,1,0:T(8,128)(2,1)}), bf16[64,88,128]{2,1,0:T(8,128)(2,1)S(1)}, u32[]{:S(2)}, u32[]{:S(2)}) async-start(bf16[64,88,128]{2,1,0:T(8,128)(2,1)} %broadcast_in_dim.31), calls=%async_computation.1 | async-start | bytes 2883584 | tf_op jit(solution)/shard_map/all_to_all | solution.py:502
  92.0 4.7 %copy-start.3 = (bf16[64,88,128]{2,1,0:T(8,128)(2,1)}, bf16[64,88,128]{2,1,0:T(8,128)(2,1)S(1)}, u32[]{:S(2)}) copy-start(bf16[64,88,128]{2,1,0:T(8,128)(2,1)S(1)} %all-to-all-done.1) | copy-start | bytes 4325380
  92.0 4.7 %collective-permute-start.3 = (bf16[5632,128]{1,0:T(8,128)(2,1)S(1)}, bf16[5632,128]{1,0:T(8,128)(2,1)S(1)}, u32[]{:S(2)}, u32[]{:S(2)}) collective-permute-start(bf16[5632,128]{1,0:T(8,128)(2,1)S(1)} %bitcast.9), channel_id=1, source_target_pairs={{0,1},{1,0},{2,3},{3,2},{4,5},{5,4},{6,7},{7,6},{8,9},{9,8},{10,11... | collective-permute-start | bytes 4325384 | tf_op jit(solution)/shard_map/ppermute | solution.py:513
  96.7 1.1 copy-start.7
